TPU v7x, 32 devices: a whole 2x2x4 slice. The times are simulated.
32 devices in a mesh: thick: 4 (over y, core), wide: 8 (over z, x).
Axes of the slice: x: 2, y: 2, z: 4, core: 2. Of those that a mesh axis runs over, the one named last changes fastest.
Arguments:
- phase_in: float32 [128, 512, 512], P('thick', 'wide'), may hold values from -1 to 1
- density_in: float32 [128, 512, 512], P('thick', 'wide'), may hold values from 0 to 1
Outputs:
- phase_out: float32 [128, 512, 512], P('thick', 'wide')
- density_out: float32 [128, 512, 512], P('thick', 'wide')
- mean_flux: float32 [], replicated
All inputs are finite; a program needn't handle non-finite values.
Results may differ from a plain program's by a relative error of at most 0.0001.
Values sent between devices are 32-bit elements; how exact they have to be, the bound alone decides.
A program may use at most 192 MiB of HBM per device.

v0:
```python
import math
import jax
import jax.numpy as jnp
from jax import lax
from jax.sharding import PartitionSpec as P

NX = 512
NY = 512
NZ = 128
DIFF_STEPS = 3
time_step = 100.0
stabilizer = 3.0
gradient_energy = 2.0
walk_step = 0.16


def with_halo(array, sides, width):
    for axis, dim in sides:
        peers, length = (lax.axis_size(axis), array.shape[dim])
        up = [(i, (i + 1) % peers) for i in range(peers)]
        down = [(j, i) for i, j in up]
        last = lax.slice_in_dim(array, length - width, length, axis=dim)
        leading = lax.slice_in_dim(array, 0, width, axis=dim)
        before = lax.ppermute(last, axis, up)
        after = lax.ppermute(leading, axis, down)
        array = jnp.concatenate([before, array, after], axis=dim)
    return array


def tables(length):
    index = jnp.arange(length, dtype=jnp.int32)
    folded = index[:, None] * index[None, :] % length
    angle = folded.astype(jnp.float32) * (2.0 * math.pi / length)
    return (jnp.cos(angle), jnp.sin(angle))


def squared_wave(index, length):
    signed = jnp.where(index < length // 2, index, index - length).astype(jnp.float32)
    return (signed * (2.0 * math.pi / length)) ** 2


def product(form, left, right):
    return jnp.einsum(form, left, right, precision=lax.Precision.HIGHEST)


def advance(density, conduct):
    centre = density[1:-1, 1:-1]
    middle = conduct[1:-1, 1:-1]

    def inflow(near_density, near_conduct):
        return 0.5 * (near_conduct + middle) * (near_density - centre)

    lower = inflow(density[:-2, 1:-1], conduct[:-2, 1:-1])
    total = lower + inflow(density[2:, 1:-1], conduct[2:, 1:-1])
    total = (
        total
        + inflow(density[1:-1, :-2], conduct[1:-1, :-2])
        + inflow(density[1:-1, 2:], conduct[1:-1, 2:])
    )
    total = (
        total
        + inflow(jnp.roll(centre, 1, 2), jnp.roll(middle, 1, 2))
        + inflow(jnp.roll(centre, -1, 2), jnp.roll(middle, -1, 2))
    )
    return (centre + walk_step * total, lower)


def per_device(phase_in, density_in):
    wide_count = lax.axis_size("wide")
    thick_count = lax.axis_size("thick")
    y_share = NY // wide_count
    x_share = NX // thick_count
    cosine_y, sine_y = tables(NY)
    cosine_x, sine_x = tables(NX)
    cosine_z, sine_z = tables(NZ)
    wave_y = squared_wave(
        lax.axis_index("wide") * y_share + jnp.arange(y_share, dtype=jnp.int32), NY
    )
    wave_x = squared_wave(
        lax.axis_index("thick") * x_share + jnp.arange(x_share, dtype=jnp.int32), NX
    )
    wave_z = squared_wave(jnp.arange(NZ, dtype=jnp.int32), NZ)
    wave = wave_y[:, None, None] + wave_z[None, :, None] + wave_x[None, None, :]
    implicit = 1.0 + time_step * stabilizer * wave + time_step * gradient_energy * wave * wave
    factor = 1.0 / (NX * NY * NZ)
    keep = (1.0 + time_step * stabilizer * wave) / implicit * factor
    drive = -time_step * wave / implicit * factor
    phase = phase_in
    chemical = phase * phase * phase - phase
    form = "fzxy,yk->fzxk"
    fields = jnp.stack([phase, chemical])
    real_part = product(form, fields, cosine_y)
    imag_part = -product(form, fields, sine_y)
    pair = (
        lax.all_to_all(real_part, "wide", split_axis=3, concat_axis=2, tiled=True),
        lax.all_to_all(imag_part, "wide", split_axis=3, concat_axis=2, tiled=True),
    )
    forward_real_part, forward_imag_part = pair
    form = "fzxy,xk->fzyk"
    out_real = product(form, forward_real_part, cosine_x) + product(form, forward_imag_part, sine_x)
    out_imag = product(form, forward_imag_part, cosine_x) - product(form, forward_real_part, sine_x)
    pair = (
        lax.all_to_all(out_real, "thick", split_axis=3, concat_axis=1, tiled=True),
        lax.all_to_all(out_imag, "thick", split_axis=3, concat_axis=1, tiled=True),
    )
    real_part, imag_part = pair
    form = "fzyk,zw->fywk"
    forward_out_real = product(form, real_part, cosine_z) + product(form, imag_part, sine_z)
    forward_out_imag = product(form, imag_part, cosine_z) - product(form, real_part, sine_z)
    real_part = forward_out_real
    imag_part = forward_out_imag
    new_real = keep * real_part[0] + drive * real_part[1]
    new_imag = keep * imag_part[0] + drive * imag_part[1]
    form = "ywk,wz->yzk"
    depth_real = product(form, new_real, cosine_z) - product(form, new_imag, sine_z)
    depth_imag = product(form, new_imag, cosine_z) + product(form, new_real, sine_z)
    real_part = lax.all_to_all(depth_real, "thick", split_axis=1, concat_axis=2, tiled=True)
    imag_part = lax.all_to_all(depth_imag, "thick", split_axis=1, concat_axis=2, tiled=True)
    form = "yzk,kx->zxy"
    out_real = product(form, real_part, cosine_x) - product(form, imag_part, sine_x)
    out_imag = product(form, imag_part, cosine_x) + product(form, real_part, sine_x)
    pair = (out_real, out_imag)
    real_part = lax.all_to_all(pair[0], "wide", split_axis=1, concat_axis=2, tiled=True)
    imag_part = lax.all_to_all(pair[1], "wide", split_axis=1, concat_axis=2, tiled=True)
    form = "zxk,ky->zxy"
    phase = product(form, real_part, cosine_y) - product(form, imag_part, sine_y)
    conduct = 0.05 + 0.95 * jax.nn.sigmoid(4.0 * phase)
    position = lax.axis_index("thick")
    final = thick_count - 1

    def pin_density(density, margin):
        depth = density.shape[0]
        layer = jnp.arange(depth, dtype=jnp.int32)[:, None, None]
        density = jnp.where((position == 0) & (layer < margin), 1.0, density)
        return jnp.where((position == final) & (layer >= depth - margin), 0.0, density)

    density = density_in
    lower = jnp.zeros_like(density)
    conduct_ext = with_halo(conduct, (("thick", 0), ("wide", 1)), 1)
    depth = conduct_ext.shape[0]
    layer = jnp.arange(depth, dtype=jnp.int32)[:, None, None]
    first = conduct_ext[1 : 1 + 1]
    last = conduct_ext[depth - 1 - 1 : depth - 1]
    conduct_ext = jnp.where((position == 0) & (layer < 1), first, conduct_ext)
    conduct_ext = jnp.where((position == final) & (layer >= depth - 1), last, conduct_ext)
    for turn in range(DIFF_STEPS):
        padded = pin_density(with_halo(density, (("thick", 0), ("wide", 1)), 1), 1)
        density, lower = advance(padded, conduct_ext)
    flux = lax.psum(jnp.sum(lower), ("thick", "wide")) / (NX * NY)
    return (phase, density, flux)


def solution(mesh):
    in_specs = (P("thick", "wide", None), P("thick", "wide", None))
    out_specs = (P("thick", "wide", None), P("thick", "wide", None), P())
    return jax.shard_map(
        per_device, mesh=mesh, in_specs=in_specs, out_specs=out_specs, check_vma=False
    )
```

profile of v0, /device:TPU:12, one launch (start us, length us, event | category | flops | bytes accessed | tf_op | source)
XLA Modules:
  0.0 1466.6 jit_solution(4611788430884908214)
XLA Ops:
  5.6 32.7 %fusion.1 = f32[2,32,64,512]{3,2,1,0:T(8,128)} fusion(f32[1,32,64,512]{3,2,1,0:T(8,128)S(1)} %fusion.5, f32[1,32,64,512]{3,2,1,0:T(8,128)S(1)} %bitcast.208), kind=kOutput, calls=%fused_computation.12 | convolution fusion | flops 12890669056 | bytes 16777216 | tf_op jit(solution)/shard_map/fzxy,yk->fzxk/dot_general | solution.py:43
  38.3 16.3 %copy.13 = f32[2,32,64,512]{2,1,0,3:T(8,128)} copy(f32[2,32,64,512]{3,2,1,0:T(8,128)} %fusion.1) | data formatting | bytes 16777216 | tf_op jit(solution)/shard_map/fzxy,yk->fzxk/dot_general | solution.py:43
  76.5 25.5 %fusion.63 = f32[2,32,64,512]{3,2,1,0:T(8,128)} fusion(f32[1,32,64,512]{3,2,1,0:T(8,128)} %copy-done.5, f32[1,32,64,512]{3,2,1,0:T(8,128)} %bitcast.207), kind=kOutput, calls=%fused_computation.115 | convolution fusion | flops 12892766208 | bytes 16777216 | tf_op jit(solution)/shard_map/fzxy,yk->fzxk/dot_general | solution.py:43
  102.0 16.8 %copy.15 = f32[2,32,64,512]{2,1,0,3:T(8,128)} copy(f32[2,32,64,512]{3,2,1,0:T(8,128)} %fusion.63) | data formatting | bytes 16777216 | tf_op jit(solution)/shard_map/neg | solution.py:93
  134.3 122.8 %all-to-all-done = f32[8,1,262144]{2,1,0:T(1,128)} async-done(((f32[8,1,262144]{2,1,0:T(1,128)}), f32[8,1,262144]{2,1,0:T(1,128)}, u32[]{:S(2)}, u32[]{:S(2)}) %all-to-all-start) | async-done | bytes 8388640 | tf_op jit(solution)/shard_map/all_to_all | solution.py:95
  265.0 26.3 %reduce = f32[8,262144]{1,0:T(8,128)} reduce(f32[8,1,262144]{2,1,0:T(1,128)} %all-to-all-done, f32[]{:T(128)} %broadcast.342), dimensions={1}, to_apply=%all_to_all.104.reduce_sub_computation | reduce | bytes 16777220 | tf_op jit(solution)/shard_map/all_to_all | solution.py:95
  291.2 15.6 %reshape.92 = f32[512,2,32,64]{3,2,1,0:T(8,128)} reshape(f32[8,262144]{1,0:T(8,128)} %reduce) | data formatting | bytes 16777216
  306.9 17.8 %copy.40 = f32[2,32,64,8,64]{2,3,4,1,0:T(8,128)} copy(f32[2,32,64,8,64]{2,1,0,4,3:T(8,128)} %bitcast.195) | data formatting | bytes 16777216 | tf_op jit(solution)/shard_map/all_to_all | solution.py:95
  338.9 25.5 %fusion.75 = f32[2,32,64,512]{3,2,1,0:T(8,128)} fusion(f32[2,32,512,64]{2,3,1,0:T(8,128)} %all_to_all.107), kind=kOutput, calls=%fused_computation.133 | convolution fusion | flops 12888571904 | bytes 16777216 | tf_op jit(solution)/shard_map/fzxy,xk->fzyk/dot_general | solution.py:43
  364.5 79.8 %all-to-all-done.1 = f32[8,1,262144]{2,1,0:T(1,128)} async-done(((f32[8,1,262144]{2,1,0:T(1,128)}), f32[8,1,262144]{2,1,0:T(1,128)}, u32[]{:S(2)}, u32[]{:S(2)}) %all-to-all-start.1) | async-done | bytes 8388640 | tf_op jit(solution)/shard_map/all_to_all | solution.py:96
  444.3 26.5 %reduce.1 = f32[8,262144]{1,0:T(8,128)} reduce(f32[8,1,262144]{2,1,0:T(1,128)} %all-to-all-done.1, f32[]{:T(128)} %broadcast.342), dimensions={1}, to_apply=%all_to_all.108.reduce_sub_computation | reduce | bytes 16777220 | tf_op jit(solution)/shard_map/all_to_all | solution.py:96
  470.8 15.6 %reshape.94 = f32[512,2,32,64]{3,2,1,0:T(8,128)} reshape(f32[8,262144]{1,0:T(8,128)} %reduce.1) | data formatting | bytes 16777216
  486.4 17.8 %copy.39 = f32[2,32,64,8,64]{2,3,4,1,0:T(8,128)} copy(f32[2,32,64,8,64]{2,1,0,4,3:T(8,128)} %bitcast.197) | data formatting | bytes 16777216 | tf_op jit(solution)/shard_map/all_to_all | solution.py:96
  518.9 26.8 %convolution_add_fusion = f32[2,32,64,512]{3,2,1,0:T(8,128)} fusion(f32[2,32,64,512]{3,2,1,0:T(8,128)} %fusion.75, f32[2,32,512,64]{2,3,1,0:T(8,128)} %all_to_all.111), kind=kOutput, calls=%fused_computation.117 | convolution fusion | flops 12890669056 | bytes 25165824 | tf_op jit(solution)/shard_map/fzxy,xk->fzyk/dot_general | solution.py:43
  545.6 16.4 %copy.17 = f32[2,32,64,512]{2,1,0,3:T(8,128)} copy(f32[2,32,64,512]{3,2,1,0:T(8,128)} %convolution_add_fusion) | data formatting | bytes 16777216 | tf_op jit(solution)/shard_map/add | solution.py:100
  582.5 24.2 %fusion.73 = f32[2,32,64,512]{3,2,1,0:T(8,128)S(1)} fusion(f32[2,32,512,64]{2,3,1,0:T(8,128)} %all_to_all.111), kind=kOutput, calls=%fused_computation.131 | convolution fusion | flops 12888571904 | bytes 16777216 | tf_op jit(solution)/shard_map/fzxy,xk->fzyk/dot_general | solution.py:43
  606.8 25.9 %convolution_subtract_fusion = f32[2,32,64,512]{3,2,1,0:T(8,128)} fusion(f32[2,32,64,512]{3,2,1,0:T(8,128)S(1)} %fusion.73, f32[2,32,512,64]{2,3,1,0:T(8,128)} %all_to_all.107), kind=kOutput, calls=%fused_computation.116 | convolution fusion | flops 12890669056 | bytes 25165824 | tf_op jit(solution)/shard_map/fzxy,xk->fzyk/dot_general | solution.py:43
  632.6 16.3 %copy.19 = f32[2,32,64,512]{2,1,0,3:T(8,128)} copy(f32[2,32,64,512]{3,2,1,0:T(8,128)} %convolution_subtract_fusion) | data formatting | bytes 16777216 | tf_op jit(solution)/shard_map/sub | solution.py:101
  681.7 28.3 %reduce.2 = f32[4,524288]{1,0:T(4,128)} reduce(f32[4,1,524288]{2,1,0:T(1,128)} %all-to-all-done.2, f32[]{:T(128)} %broadcast.342), dimensions={1}, to_apply=%all_to_all.112.reduce_sub_computation | reduce | bytes 16777220 | tf_op jit(solution)/shard_map/all_to_all | solution.py:103
  709.9 16.8 %reshape.96 = f32[512,2,32,64]{3,2,1,0:T(8,128)} reshape(f32[4,524288]{1,0:T(4,128)} %reduce.2) | data formatting | bytes 16777216
  726.7 15.9 %copy.18 = f32[2,32,64,4,128]{4,1,3,2,0:T(8,128)} copy(f32[2,32,64,4,128]{2,1,0,4,3:T(8,128)} %bitcast.193) | data formatting | bytes 16777216 | tf_op jit(solution)/shard_map/all_to_all | solution.py:103
  754.8 18.2 %all-to-all-done.3 = f32[4,1,524288]{2,1,0:T(1,128)} async-done(((f32[4,1,524288]{2,1,0:T(1,128)}), f32[4,1,524288]{2,1,0:T(1,128)}, u32[]{:S(2)}, u32[]{:S(2)}) %all-to-all-start.3) | async-done | bytes 8388640 | tf_op jit(solution)/shard_map/all_to_all | solution.py:104
  773.1 28.6 %reduce.3 = f32[4,524288]{1,0:T(4,128)} reduce(f32[4,1,524288]{2,1,0:T(1,128)} %all-to-all-done.3, f32[]{:T(128)} %broadcast.342), dimensions={1}, to_apply=%all_to_all.116.reduce_sub_computation | reduce | bytes 16777220 | tf_op jit(solution)/shard_map/all_to_all | solution.py:104
  801.7 16.8 %reshape.98 = f32[512,2,32,64]{3,2,1,0:T(8,128)} reshape(f32[4,524288]{1,0:T(4,128)} %reduce.3) | data formatting | bytes 16777216
  818.5 15.8 %copy.20 = f32[2,32,64,4,128]{4,1,3,2,0:T(8,128)} copy(f32[2,32,64,4,128]{2,1,0,4,3:T(8,128)} %bitcast.194) | data formatting | bytes 16777216 | tf_op jit(solution)/shard_map/all_to_all | solution.py:104
  913.3 24.9 %all-to-all-done.4 = f32[64,128,128]{2,0,1:T(8,128)} async-done(((f32[64,128,128]{2,0,1:T(8,128)}), f32[64,128,128]{2,0,1:T(8,128)}, u32[]{:S(2)}, u32[]{:S(2)}) %all-to-all-start.4) | async-done | bytes 4194336 | tf_op jit(solution)/shard_map/all_to_all | solution.py:117
  972.5 19.0 %all-to-all-done.5 = f32[64,128,128]{2,0,1:T(8,128)} async-done(((f32[64,128,128]{2,0,1:T(8,128)}), f32[64,128,128]{2,0,1:T(8,128)}, u32[]{:S(2)}, u32[]{:S(2)}) %all-to-all-start.5) | async-done | bytes 4194336 | tf_op jit(solution)/shard_map/all_to_all | solution.py:118
  1090.1 46.9 %all-to-all-done.6 = f32[8,1,131072]{2,1,0:T(1,128)} async-done(((f32[8,1,131072]{2,1,0:T(1,128)}), f32[8,1,131072]{2,1,0:T(1,128)}, u32[]{:S(2)}, u32[]{:S(2)}) %all-to-all-start.6) | async-done | bytes 4194336 | tf_op jit(solution)/shard_map/all_to_all | solution.py:123
  1206.3 28.0 %all-to-all-done.7 = f32[8,1,131072]{2,1,0:T(1,128)} async-done(((f32[8,1,131072]{2,1,0:T(1,128)}), f32[8,1,131072]{2,1,0:T(1,128)}, u32[]{:S(2)}, u32[]{:S(2)}) %all-to-all-start.7) | async-done | bytes 4194336 | tf_op jit(solution)/shard_map/all_to_all | solution.py:124
  1276.3 24.5 %multiply_add_fusion = (f32[32,64,512]{2,1,0:T(8,128)S(1)}, f32[32,64,512]{2,1,0:T(8,128)}) fusion(f32[32,64,512]{2,1,0:T(8,128)} %fusion.80, f32[32,64,512]{2,1,0:T(8,128)} %all_to_all.135), kind=kOutput, calls=%fused_computation.110 | convolution fusion | flops 6453460992 | bytes 16777216 | tf_op jit(solution)/shard_map/zxk,ky->zxy/dot_general | solution.py:43
  1334.5 16.4 %fusion.39 = (f32[32,64,512]{2,1,0:T(8,128)}, f32[32,64,512]{2,1,0:T(8,128)}, f32[32,64,512]{2,1,0:T(8,128)}, f32[32,64,512]{2,1,0:T(8,128)}) fusion(f32[34,66,512]{2,1,0:T(8,128)S(1)} %get-tuple-element.44, f32[32,64,511]{2,1,0:T(8,128)} %get-tuple-element.49, f32[32,64,1]{2,1,0:T(8,128)} %get-tuple-element.47, f32[32,64,1]{2,1,0:T(8,128)} %get-tuple-element.48, ...), kind=kLoop, calls=%fused_computation.65 | loop fusion | flops 36700160 | bytes 75497472 | tf_op jit(solution)/shard_map/add | solution.py:65
  1421.5 42.8 %psum.7 = f32[]{:T(128)} all-reduce(f32[]{:T(128)} %get-tuple-element.7), channel_id=1, replica_groups=mesh['thick'=4,'wide'=8] {'thick','wide'}, use_global_device_ids=true, to_apply=%region_1.2 | all-reduce | flops 1 | bytes 8 | tf_op jit(solution)/shard_map/psum | solution.py:149
  (140 shorter events, 571.6 us)
Async XLA Ops:
  70.0 187.1 %all-to-all-start = ((f32[8,1,262144]{2,1,0:T(1,128)}), f32[8,1,262144]{2,1,0:T(1,128)}, u32[]{:S(2)}, u32[]{:S(2)}) async-start(f32[8,1,262144]{2,1,0:T(1,128)} %reshape.91), calls=%async_computation | async-start | bytes 16777216 | tf_op jit(solution)/shard_map/all_to_all | solution.py:95
  257.1 187.2 %all-to-all-start.1 = ((f32[8,1,262144]{2,1,0:T(1,128)}), f32[8,1,262144]{2,1,0:T(1,128)}, u32[]{:S(2)}, u32[]{:S(2)}) async-start(f32[8,1,262144]{2,1,0:T(1,128)} %reshape.93), calls=%async_computation.1 | async-start | bytes 16777216 | tf_op jit(solution)/shard_map/all_to_all | solution.py:96
  576.4 97.7 %all-to-all-start.2 = ((f32[4,1,524288]{2,1,0:T(1,128)}), f32[4,1,524288]{2,1,0:T(1,128)}, u32[]{:S(2)}, u32[]{:S(2)}) async-start(f32[4,1,524288]{2,1,0:T(1,128)} %reshape.95), calls=%async_computation.2 | async-start | bytes 16777216 | tf_op jit(solution)/shard_map/all_to_all | solution.py:103
  674.1 99.0 %all-to-all-start.3 = ((f32[4,1,524288]{2,1,0:T(1,128)}), f32[4,1,524288]{2,1,0:T(1,128)}, u32[]{:S(2)}, u32[]{:S(2)}) async-start(f32[4,1,524288]{2,1,0:T(1,128)} %reshape.97), calls=%async_computation.3 | async-start | bytes 16777216 | tf_op jit(solution)/shard_map/all_to_all | solution.py:104
  834.3 23.7 %slice-start = ((s8[8388608]{0:T(1024)(128)(4,1)}), s8[4194304]{0:T(1024)(128)(4,1)S(1)}, s32[]{:S(2)}) async-start(s8[8388608]{0:T(1024)(128)(4,1)} %bitcast.184), calls=%async_computation.8 | async-start | bytes 8388608
  845.6 12.4 slice-start.1
  885.1 53.1 %all-to-all-start.4 = ((f32[64,128,128]{2,0,1:T(8,128)}), f32[64,128,128]{2,0,1:T(8,128)}, u32[]{:S(2)}, u32[]{:S(2)}) async-start(f32[64,128,128]{2,0,1:T(8,128)} %copy.21), calls=%async_computation.4 | async-start | bytes 8388608 | tf_op jit(solution)/shard_map/all_to_all | solution.py:117
  938.2 53.3 %all-to-all-start.5 = ((f32[64,128,128]{2,0,1:T(8,128)}), f32[64,128,128]{2,0,1:T(8,128)}, u32[]{:S(2)}, u32[]{:S(2)}) async-start(f32[64,128,128]{2,0,1:T(8,128)} %copy.23), calls=%async_computation.5 | async-start | bytes 8388608 | tf_op jit(solution)/shard_map/all_to_all | solution.py:118
  1038.6 98.4 %all-to-all-start.6 = ((f32[8,1,131072]{2,1,0:T(1,128)}), f32[8,1,131072]{2,1,0:T(1,128)}, u32[]{:S(2)}, u32[]{:S(2)}) async-start(f32[8,1,131072]{2,1,0:T(1,128)} %reshape.99), calls=%async_computation.6 | async-start | bytes 8388608 | tf_op jit(solution)/shard_map/all_to_all | solution.py:123
  1046.0 12.7 copy-start.1
  1137.0 97.2 %all-to-all-start.7 = ((f32[8,1,131072]{2,1,0:T(1,128)}), f32[8,1,131072]{2,1,0:T(1,128)}, u32[]{:S(2)}, u32[]{:S(2)}) async-start(f32[8,1,131072]{2,1,0:T(1,128)} %reshape.101), calls=%async_computation.7 | async-start | bytes 8388608 | tf_op jit(solution)/shard_map/all_to_all | solution.py:124
  1145.0 4.4 collective-permute-start
  1145.1 157.1 %collective-permute-start.1 = (f32[1,64,512]{2,1,0:T(8,128)S(1)}, f32[1,64,512]{2,1,0:T(8,128)S(1)}, u32[]{:S(2)}, u32[]{:S(2)}) collective-permute-start(f32[1,64,512]{2,1,0:T(8,128)S(1)} %get-tuple-element.41), channel_id=1, source_target_pairs={{8,0},{16,8},{24,16},{0,24},{9,1},{17,9},{25,17},{1,25},{10,2},{18... | collective-permute-start | bytes 393224 | tf_op jit(solution)/shard_map/ppermute | solution.py:25
  1268.7 32.9 %slice-start.2 = ((s8[4456448]{0:T(1024)(128)(4,1)}), s8[262144]{0:T(1024)(128)(4,1)S(1)}, s32[]{:S(2)}) async-start(s8[4456448]{0:T(1024)(128)(4,1)} %bitcast.209), calls=%async_computation.10 | async-start | bytes 524288
  1276.2 25.4 %slice-start.3 = ((s8[4456448]{0:T(1024)(128)(4,1)}), s8[4194304]{0:T(1024)(128)(4,1)S(1)}, s32[]{:S(2)}) async-start(s8[4456448]{0:T(1024)(128)(4,1)} %bitcast.209), calls=%async_computation.11 | async-start | bytes 8388608
  1276.3 25.4 %copy-start.9 = (f32[32,64,512]{2,1,0:T(8,128)S(1)}, f32[32,64,512]{2,1,0:T(8,128)}, u32[]{:S(2)}) copy-start(f32[32,64,512]{2,1,0:T(8,128)} %param.3) | copy-start | bytes 12582916
  1300.7 4.6 collective-permute-start.5
  1301.7 5.1 collective-permute-start.4
  1302.2 14.2 copy-start.8
  1306.9 6.2 collective-permute-start.7
  1310.0 5.3 collective-permute-start.6
  1310.2 6.3 collective-permute-start.3
  1313.1 5.2 collective-permute-start.2
  1350.9 17.4 %copy-start.2 = (f32[32,64,512]{2,1,0:T(8,128)S(1)}, f32[32,64,512]{2,1,0:T(8,128)}, u32[]{:S(2)}) copy-start(f32[32,64,512]{2,1,0:T(8,128)} %get-tuple-element.3) | copy-start | bytes 12582916
  1352.1 3.7 collective-permute-start.9
  1352.1 5.1 collective-permute-start.8
  1358.6 4.7 collective-permute-start.11
  1361.3 7.0 collective-permute-start.10
  1388.2 3.7 collective-permute-start.13
  1388.3 5.1 collective-permute-start.12
  1393.5 4.4 collective-permute-start.15
  1395.5 5.2 collective-permute-start.14
  (6 other events, 39.5 us)
where the time goes:
time: 1480 us; the launch traced here: 1470 us
  local copies, waits for them, and re-layouts  443 us (30%)
  waiting for transfers between devices  383 us (26%)
  matrix products  329 us (22%)
  other arithmetic  196 us (13%)
  starting transfers between devices  69.8 us (5%)
  blocking collectives  42.8 us (3%)
    dot_general x20, matrix products, product(): return jnp.einsum(form, left, right, precision=lax.Precision.HIGHEST)  329 us
    unnamed x42, local copies, waits for them, and re-layouts  165 us
    all_to_all x1, waiting for transfers between devices, per_device(): lax.all_to_all(real_part, 'wide', split_axis=3, concat_axis=2, tiled=True)  123 us
    all_to_all x1, waiting for transfers between devices, per_device(): lax.all_to_all(imag_part, 'wide', split_axis=3, concat_axis=2, tiled=True)  79.8 us
    all_to_all x1, waiting for transfers between devices, per_device(): lax.all_to_all(pair[0], 'wide', split_axis=1, concat_axis=2, tiled=True)  46.9 us
    psum x1, blocking collectives, per_device(): flux = lax.psum(jnp.sum(lower), ('thick', 'wide')) / (NX * NY)  42.8 us
    all_to_all x3, local copies, waits for them, and re-layouts, per_device(): lax.all_to_all(real_part, 'wide', split_axis=3, concat_axis=2, tiled=True)  32.6 us
    all_to_all x2, local copies, waits for them, and re-layouts, per_device(): lax.all_to_all(imag_part, 'wide', split_axis=3, concat_axis=2, tiled=True)  32.5 us
  transfers between devices with their start and end apart: 24, of which 21 were waited for; matrix products, arithmetic and copies ran while one was open for 34% of the time, Pallas kernels for 0%

commit v1 on v0

--- a/solution.py
+++ b/solution.py
@@ -12,6 +12,28 @@
 stabilizer = 3.0
 gradient_energy = 2.0
 walk_step = 0.16
+
+
+def split_up(shard, dim, count):
+    before, after = (shard.shape[:dim], shard.shape[dim + 1 :])
+    return jnp.moveaxis(shard.reshape(*before, count, -1, *after), dim, 0)
+
+
+def laid_out(pieces, dim):
+    pieces = jnp.moveaxis(pieces, 0, dim)
+    lengths = pieces.shape
+    return pieces.reshape(*lengths[:dim], lengths[dim] * lengths[dim + 1], *lengths[dim + 2 :])
+
+
+def sent_to_each(x, axis, split_dim, concat_dim):
+    devices, position = (lax.axis_size(axis), lax.axis_index(axis))
+    blocks = split_up(x, split_dim, devices)
+    outs = [blocks[position]]
+    for step in range(1, devices):
+        sent = blocks[(position + step) % devices]
+        outs.append(lax.ppermute(sent, axis, [(i, (i + step) % devices) for i in range(devices)]))
+    blocks = jnp.stack(outs)[(position - jnp.arange(devices)) % devices]
+    return laid_out(blocks, concat_dim)
 
 
 def with_halo(array, sides, width):
@@ -93,7 +115,7 @@
     imag_part = -product(form, fields, sine_y)
     pair = (
         lax.all_to_all(real_part, "wide", split_axis=3, concat_axis=2, tiled=True),
-        lax.all_to_all(imag_part, "wide", split_axis=3, concat_axis=2, tiled=True),
+        sent_to_each(imag_part, "wide", 3, 2),
     )
     forward_real_part, forward_imag_part = pair
     form = "fzxy,xk->fzyk"

time: 1480 us -> 1730 us (1.17)
  waiting for transfers between devices: 383 us -> 603 us
  local copies, waits for them, and re-layouts: 443 us -> 494 us
  other arithmetic: 196 us -> 168 us
    ppermute x0 -> x7, waiting for transfers between devices: none -> 419 us  [sent_to_each(): lax.ppermute(sent, axis, [(i, (i + step) % devices) for i in range(device...]
    all_to_all x1, waiting for transfers between devices: 123 us -> 0.01 us  [per_device(): lax.all_to_all(real_part, 'wide', split_axis=3, concat_axis=2, tiled=True)]
    all_to_all x1 -> x0, waiting for transfers between devices: 79.8 us -> none  [per_device(): lax.all_to_all(imag_part, 'wide', split_axis=3, concat_axis=2, tiled=True)]
    another operation x0 -> x2, local copies, waits for them, and re-layouts: none -> 60.5 us
    all_to_all x2 -> x0, local copies, waits for them, and re-layouts: 32.5 us -> none  [per_device(): lax.all_to_all(imag_part, 'wide', split_axis=3, concat_axis=2, tiled=True)]
    reshape x0 -> x2, local copies, waits for them, and re-layouts: none -> 27.1 us  [the longest x1 14.2 us: laid_out(): pieces.reshape(*lengths[:dim], lengths[dim] * lengths[dim + 1], *lengths[...]
    all_to_all x1 -> x0, other arithmetic: 26.5 us -> none  [per_device(): lax.all_to_all(imag_part, 'wide', split_axis=3, concat_axis=2, tiled=True)]
    all_to_all x1, waiting for transfers between devices: 28 us -> 46.7 us  [per_device(): lax.all_to_all(pair[1], 'wide', split_axis=1, concat_axis=2, tiled=True)]
  transfers between devices with their start and end apart: 24 -> 30, of which waited for: 21 -> 26; matrix products, arithmetic and copies ran while one was open for 34% -> 31% of each run, Pallas kernels for 0% -> 0%
where the time goes in v1:
time: 1730 us; the launch traced here: 1720 us
  waiting for transfers between devices  603 us (35%)
  local copies, waits for them, and re-layouts  494 us (29%)
  matrix products  326 us (19%)
  other arithmetic  168 us (10%)
  starting transfers between devices  83.2 us (5%)
  blocking collectives  46.5 us (3%)
    ppermute x7, waiting for transfers between devices, sent_to_each(): lax.ppermute(sent, axis, [(i, (i + step) % devices) for i in range(device...  419 us
    dot_general x20, matrix products, product(): return jnp.einsum(form, left, right, precision=lax.Precision.HIGHEST)  326 us
    unnamed x51, local copies, waits for them, and re-layouts  146 us
    another operation x1, local copies, waits for them, and re-layouts  59.1 us
    all_to_all x1, waiting for transfers between devices, per_device(): lax.all_to_all(pair[1], 'wide', split_axis=1, concat_axis=2, tiled=True)  46.7 us
    psum x1, blocking collectives, per_device(): flux = lax.psum(jnp.sum(lower), ('thick', 'wide')) / (NX * NY)  46.5 us
    all_to_all x1, waiting for transfers between devices, per_device(): lax.all_to_all(pair[0], 'wide', split_axis=1, concat_axis=2, tiled=True)  42.1 us
  transfers between devices with their start and end apart: 30, of which 26 were waited for; matrix products, arithmetic and copies ran while one was open for 31% of the time, Pallas kernels for 0%

profile of v1, /device:TPU:12, one launch (start us, length us, event | category | flops | bytes accessed | tf_op | source)
XLA Modules:
  0.0 1724.4 jit_solution(11380762123890232220)
XLA Ops:
  5.6 32.8 %fusion.1 = f32[2,32,64,512]{3,2,1,0:T(8,128)} fusion(f32[1,32,64,512]{3,2,1,0:T(8,128)S(1)} %fusion.5, f32[1,32,64,512]{3,2,1,0:T(8,128)S(1)} %bitcast.227), kind=kOutput, calls=%fused_computation.12 | convolution fusion | flops 12890669056 | bytes 16777216 | tf_op jit(solution)/shard_map/fzxy,yk->fzxk/dot_general | solution.py:65
  38.3 16.3 copy.27
  76.9 25.6 %fusion.63 = f32[2,32,64,512]{3,2,1,0:T(8,128)} fusion(f32[1,32,64,512]{3,2,1,0:T(8,128)} %copy-done.5, f32[1,32,64,512]{3,2,1,0:T(8,128)} %bitcast.226), kind=kOutput, calls=%fused_computation.115 | convolution fusion | flops 12892766208 | bytes 16777216 | tf_op jit(solution)/shard_map/fzxy,yk->fzxk/dot_general | solution.py:65
  115.4 59.1 %constant_dynamic-slice_fusion = (f32[2,32,64,1,64]{4,3,2,1,0:T(1,128)}, f32[2,32,64,1,64]{4,3,2,1,0:T(1,128)}, f32[2,32,64,1,64]{4,3,2,1,0:T(1,128)}, f32[2,32,...) fusion(f32[2,32,64,8,64]{4,3,2,1,0:T(8,128)} %reshape.153, ...), kind=kLoop, calls=%fused_computation.218 | loop fusion | bytes 16777248 | tf_op jit(solution)/shard_map/dynamic-slice.7
  184.3 76.1 %collective-permute-done = f32[2,32,64,64]{3,2,1,0:T(8,128)S(1)} collective-permute-done((f32[2,32,64,64]{3,2,1,0:T(8,128)}, f32[2,32,64,64]{3,2,1,0:T(8,128)S(1)}, u32[]{:S(2)}, u32[]{:S(2)}) %collective-permute-start) | collective-permute-done | bytes 1048608 | tf_op jit(solution)/shard_map/ppermute | solution.py:34
  264.8 38.6 %collective-permute-done.1 = f32[2,32,64,64]{3,2,1,0:T(8,128)S(1)} collective-permute-done((f32[2,32,64,64]{3,2,1,0:T(8,128)}, f32[2,32,64,64]{3,2,1,0:T(8,128)S(1)}, u32[]{:S(2)}, u32[]{:S(2)}) %collective-permute-start.1) | collective-permute-done | bytes 1048608 | tf_op jit(solution)/shard_map/ppermute | solution.py:34
  309.7 217.4 %collective-permute-done.2 = f32[2,32,64,64]{3,2,1,0:T(8,128)S(1)} collective-permute-done((f32[2,32,64,64]{3,2,1,0:T(8,128)}, f32[2,32,64,64]{3,2,1,0:T(8,128)S(1)}, u32[]{:S(2)}, u32[]{:S(2)}) %collective-permute-start.2) | collective-permute-done | bytes 1048608 | tf_op jit(solution)/shard_map/ppermute | solution.py:34
  528.7 43.4 %collective-permute-done.3 = f32[2,32,64,64]{3,2,1,0:T(8,128)S(1)} collective-permute-done((f32[2,32,64,64]{3,2,1,0:T(8,128)}, f32[2,32,64,64]{3,2,1,0:T(8,128)S(1)}, u32[]{:S(2)}, u32[]{:S(2)}) %collective-permute-start.3) | collective-permute-done | bytes 1048608 | tf_op jit(solution)/shard_map/ppermute | solution.py:34
  573.6 43.4 %collective-permute-done.4 = f32[2,32,64,64]{3,2,1,0:T(8,128)S(1)} collective-permute-done((f32[2,32,64,64]{3,2,1,0:T(8,128)}, f32[2,32,64,64]{3,2,1,0:T(8,128)S(1)}, u32[]{:S(2)}, u32[]{:S(2)}) %collective-permute-start.4) | collective-permute-done | bytes 1048608 | tf_op jit(solution)/shard_map/ppermute | solution.py:34
  635.2 17.5 %copy.29 = f32[2,32,8,64,64]{3,2,4,1,0:T(8,128)} copy(f32[2,32,8,64,64]{4,3,1,0,2:T(8,128)} %bitcast.215) | data formatting | bytes 16777216 | tf_op jit(solution)/shard_map/transpose | solution.py:23
  666.9 25.7 %fusion.73 = f32[2,32,64,512]{3,2,1,0:T(8,128)} fusion(f32[2,32,512,64]{2,3,1,0:T(8,128)} %reshape.154), kind=kOutput, calls=%fused_computation.138 | convolution fusion | flops 12888571904 | bytes 16777216 | tf_op jit(solution)/shard_map/fzxy,xk->fzyk/dot_general | solution.py:65
  693.0 26.7 %reduce = f32[8,262144]{1,0:T(8,128)} reduce(f32[8,1,262144]{2,1,0:T(1,128)} %all-to-all-done, f32[]{:T(128)} %broadcast.418), dimensions={1}, to_apply=%all_to_all.91.reduce_sub_computation | reduce | bytes 16777220 | tf_op jit(solution)/shard_map/all_to_all | solution.py:117
  735.4 17.8 %copy.51 = f32[2,32,64,8,64]{2,3,4,1,0:T(8,128)} copy(f32[2,32,64,8,64]{2,1,0,4,3:T(8,128)} %bitcast.216) | data formatting | bytes 16777216 | tf_op jit(solution)/shard_map/all_to_all | solution.py:117
  767.6 26.9 %convolution_subtract_fusion = f32[2,32,64,512]{3,2,1,0:T(8,128)} fusion(f32[2,32,64,512]{3,2,1,0:T(8,128)} %fusion.73, f32[2,32,512,64]{2,3,1,0:T(8,128)} %all_to_all.94), kind=kOutput, calls=%fused_computation.116 | convolution fusion | flops 12890669056 | bytes 25165824 | tf_op jit(solution)/shard_map/fzxy,xk->fzyk/dot_general | solution.py:65
  794.4 16.7 copy.32
  831.6 24.2 %fusion.75 = f32[2,32,64,512]{3,2,1,0:T(8,128)S(1)} fusion(f32[2,32,512,64]{2,3,1,0:T(8,128)} %all_to_all.94), kind=kOutput, calls=%fused_computation.140 | convolution fusion | flops 12888571904 | bytes 16777216 | tf_op jit(solution)/shard_map/fzxy,xk->fzyk/dot_general | solution.py:65
  855.8 25.8 %convolution_add_fusion = f32[2,32,64,512]{3,2,1,0:T(8,128)} fusion(f32[2,32,64,512]{3,2,1,0:T(8,128)S(1)} %fusion.75, f32[2,32,512,64]{2,3,1,0:T(8,128)} %reshape.154), kind=kOutput, calls=%fused_computation.117 | convolution fusion | flops 12890669056 | bytes 25165824 | tf_op jit(solution)/shard_map/fzxy,xk->fzyk/dot_general | solution.py:65
  881.6 16.3 copy.30
  930.7 28.3 %reduce.2 = f32[4,524288]{1,0:T(4,128)} reduce(f32[4,1,524288]{2,1,0:T(1,128)} %all-to-all-done.2, f32[]{:T(128)} %broadcast.418), dimensions={1}, to_apply=%all_to_all.99.reduce_sub_computation | reduce | bytes 16777220 | tf_op jit(solution)/shard_map/all_to_all | solution.py:126
  959.0 16.8 reshape.176
  975.9 16.2 copy.33
  1004.2 18.0 %all-to-all-done.1 = f32[4,1,524288]{2,1,0:T(1,128)} async-done(((f32[4,1,524288]{2,1,0:T(1,128)}), f32[4,1,524288]{2,1,0:T(1,128)}, u32[]{:S(2)}, u32[]{:S(2)}) %all-to-all-start.1) | async-done | bytes 8388640 | tf_op jit(solution)/shard_map/all_to_all | solution.py:125
  1022.1 28.4 %reduce.1 = f32[4,524288]{1,0:T(4,128)} reduce(f32[4,1,524288]{2,1,0:T(1,128)} %all-to-all-done.1, f32[]{:T(128)} %broadcast.418), dimensions={1}, to_apply=%all_to_all.95.reduce_sub_computation | reduce | bytes 16777220 | tf_op jit(solution)/shard_map/all_to_all | solution.py:125
  1050.6 16.8 reshape.174
  1067.4 15.7 copy.31
  1162.0 24.9 %all-to-all-done.4 = f32[64,128,128]{2,0,1:T(8,128)} async-done(((f32[64,128,128]{2,0,1:T(8,128)}), f32[64,128,128]{2,0,1:T(8,128)}, u32[]{:S(2)}, u32[]{:S(2)}) %all-to-all-start.4) | async-done | bytes 4194336 | tf_op jit(solution)/shard_map/all_to_all | solution.py:140
  1221.7 18.6 %all-to-all-done.3 = f32[64,128,128]{2,0,1:T(8,128)} async-done(((f32[64,128,128]{2,0,1:T(8,128)}), f32[64,128,128]{2,0,1:T(8,128)}, u32[]{:S(2)}, u32[]{:S(2)}) %all-to-all-start.3) | async-done | bytes 4194336 | tf_op jit(solution)/shard_map/all_to_all | solution.py:139
  1339.2 46.7 %all-to-all-done.6 = f32[8,1,131072]{2,1,0:T(1,128)} async-done(((f32[8,1,131072]{2,1,0:T(1,128)}), f32[8,1,131072]{2,1,0:T(1,128)}, u32[]{:S(2)}, u32[]{:S(2)}) %all-to-all-start.6) | async-done | bytes 4194336 | tf_op jit(solution)/shard_map/all_to_all | solution.py:146
  1441.0 42.1 %all-to-all-done.5 = f32[8,1,131072]{2,1,0:T(1,128)} async-done(((f32[8,1,131072]{2,1,0:T(1,128)}), f32[8,1,131072]{2,1,0:T(1,128)}, u32[]{:S(2)}, u32[]{:S(2)}) %all-to-all-start.5) | async-done | bytes 4194336 | tf_op jit(solution)/shard_map/all_to_all | solution.py:145
  1538.5 21.8 %multiply_add_fusion = (f32[32,64,512]{2,1,0:T(8,128)S(1)}, f32[32,64,512]{2,1,0:T(8,128)}) fusion(f32[32,64,512]{2,1,0:T(8,128)S(1)} %fusion.80, f32[32,64,512]{2,1,0:T(8,128)S(1)} %copy-done.9), kind=kOutput, calls=%fused_computation.110 | convolution fusion | flops 6453460992 | bytes 16777216 | tf_op jit(solution)/shard_map/zxk,ky->zxy/dot_general | solution.py:65
  1591.5 16.5 fusion.39
  1675.9 46.5 %psum.7 = f32[]{:T(128)} all-reduce(f32[]{:T(128)} %get-tuple-element.15), channel_id=1, replica_groups=mesh['thick'=4,'wide'=8] {'thick','wide'}, use_global_device_ids=true, to_apply=%region_1.2 | all-reduce | flops 1 | bytes 8 | tf_op jit(solution)/shard_map/psum | solution.py:171
  (165 shorter events, 613.8 us)
Async XLA Ops:
  70.0 622.5 %all-to-all-start = ((f32[8,1,262144]{2,1,0:T(1,128)}), f32[8,1,262144]{2,1,0:T(1,128)}, u32[]{:S(2)}, u32[]{:S(2)}) async-start(f32[8,1,262144]{2,1,0:T(1,128)} %reshape.171), calls=%async_computation | async-start | bytes 16777216 | tf_op jit(solution)/shard_map/all_to_all | solution.py:117
  174.5 85.9 %copy-start.11 = (f32[2,32,64,1,64]{4,3,2,1,0:T(1,128)S(1)}, f32[2,32,64,1,64]{4,3,2,1,0:T(1,128)}, u32[]{:S(2)}) copy-start(f32[2,32,64,1,64]{4,3,2,1,0:T(1,128)} %get-tuple-element.8) | copy-start | bytes 3145732
  174.5 85.9 %collective-permute-start = (f32[2,32,64,64]{3,2,1,0:T(8,128)}, f32[2,32,64,64]{3,2,1,0:T(8,128)S(1)}, u32[]{:S(2)}, u32[]{:S(2)}) collective-permute-start(f32[2,32,64,64]{3,2,1,0:T(8,128)} %bitcast.237), channel_id=1, source_target_pairs={{0,1},{1,2},{2,3},{3,4},{4,5},{5,6},{6,7},{7,0},{8,9},{9,10},{10,1... | collective-permute-start | bytes 3145736 | tf_op jit(solution)/shard_map/ppermute | solution.py:34
  176.1 127.3 %collective-permute-start.1 = (f32[2,32,64,64]{3,2,1,0:T(8,128)}, f32[2,32,64,64]{3,2,1,0:T(8,128)S(1)}, u32[]{:S(2)}, u32[]{:S(2)}) collective-permute-start(f32[2,32,64,64]{3,2,1,0:T(8,128)} %bitcast.236), channel_id=1, source_target_pairs={{0,2},{1,3},{2,4},{3,5},{4,6},{5,7},{6,0},{7,1},{8,10},{9,11},{10,... | collective-permute-start | bytes 3145736 | tf_op jit(solution)/shard_map/ppermute | solution.py:34
  177.5 349.6 %collective-permute-start.2 = (f32[2,32,64,64]{3,2,1,0:T(8,128)}, f32[2,32,64,64]{3,2,1,0:T(8,128)S(1)}, u32[]{:S(2)}, u32[]{:S(2)}) collective-permute-start(f32[2,32,64,64]{3,2,1,0:T(8,128)} %bitcast.235), channel_id=1, source_target_pairs={{0,3},{1,4},{2,5},{3,6},{4,7},{5,0},{6,1},{7,2},{8,11},{9,12},{10,... | collective-permute-start | bytes 3145736 | tf_op jit(solution)/shard_map/ppermute | solution.py:34
  178.5 393.6 %collective-permute-start.3 = (f32[2,32,64,64]{3,2,1,0:T(8,128)}, f32[2,32,64,64]{3,2,1,0:T(8,128)S(1)}, u32[]{:S(2)}, u32[]{:S(2)}) collective-permute-start(f32[2,32,64,64]{3,2,1,0:T(8,128)} %bitcast.234), channel_id=1, source_target_pairs={{0,4},{1,5},{2,6},{3,7},{4,0},{5,1},{6,2},{7,3},{8,12},{9,13},{10,... | collective-permute-start | bytes 3145736 | tf_op jit(solution)/shard_map/ppermute | solution.py:34
  181.3 435.6 %collective-permute-start.4 = (f32[2,32,64,64]{3,2,1,0:T(8,128)}, f32[2,32,64,64]{3,2,1,0:T(8,128)S(1)}, u32[]{:S(2)}, u32[]{:S(2)}) collective-permute-start(f32[2,32,64,64]{3,2,1,0:T(8,128)} %bitcast.233), channel_id=1, source_target_pairs={{0,5},{1,6},{2,7},{3,0},{4,1},{5,2},{6,3},{7,4},{8,13},{9,14},{10,... | collective-permute-start | bytes 3145736 | tf_op jit(solution)/shard_map/ppermute | solution.py:34
  182.8 120.6 %copy-start.10 = (f32[2,32,64,1,64]{4,3,2,1,0:T(1,128)S(1)}, f32[2,32,64,1,64]{4,3,2,1,0:T(1,128)}, u32[]{:S(2)}) copy-start(f32[2,32,64,1,64]{4,3,2,1,0:T(1,128)} %get-tuple-element.7) | copy-start | bytes 3145732
  260.4 358.1 %collective-permute-start.5 = (f32[2,32,64,64]{3,2,1,0:T(8,128)S(1)}, f32[2,32,64,64]{3,2,1,0:T(8,128)S(1)}, u32[]{:S(2)}, u32[]{:S(2)}) collective-permute-start(f32[2,32,64,64]{3,2,1,0:T(8,128)S(1)} %bitcast.232), channel_id=1, source_target_pairs={{0,6},{1,7},{2,0},{3,1},{4,2},{5,3},{6,4},{7,5},{8,14},{9,15},{10,... | collective-permute-start | bytes 3145736 | tf_op jit(solution)/shard_map/ppermute | solution.py:34
  303.4 316.5 %collective-permute-start.6 = (f32[2,32,64,64]{3,2,1,0:T(8,128)S(1)}, f32[2,32,64,64]{3,2,1,0:T(8,128)S(1)}, u32[]{:S(2)}, u32[]{:S(2)}) collective-permute-start(f32[2,32,64,64]{3,2,1,0:T(8,128)S(1)} %bitcast.231), channel_id=1, source_target_pairs={{0,7},{1,0},{2,1},{3,2},{4,3},{5,4},{6,5},{7,6},{8,15},{9,8},{10,9... | collective-permute-start | bytes 3145736 | tf_op jit(solution)/shard_map/ppermute | solution.py:34
  825.5 97.7 %all-to-all-start.2 = ((f32[4,1,524288]{2,1,0:T(1,128)}), f32[4,1,524288]{2,1,0:T(1,128)}, u32[]{:S(2)}, u32[]{:S(2)}) async-start(f32[4,1,524288]{2,1,0:T(1,128)} %reshape.175), calls=%async_computation.2 | async-start | bytes 16777216 | tf_op jit(solution)/shard_map/all_to_all | solution.py:126
  923.1 99.0 %all-to-all-start.1 = ((f32[4,1,524288]{2,1,0:T(1,128)}), f32[4,1,524288]{2,1,0:T(1,128)}, u32[]{:S(2)}, u32[]{:S(2)}) async-start(f32[4,1,524288]{2,1,0:T(1,128)} %reshape.173), calls=%async_computation.1 | async-start | bytes 16777216 | tf_op jit(solution)/shard_map/all_to_all | solution.py:125
  1133.9 53.1 %all-to-all-start.4 = ((f32[64,128,128]{2,0,1:T(8,128)}), f32[64,128,128]{2,0,1:T(8,128)}, u32[]{:S(2)}, u32[]{:S(2)}) async-start(f32[64,128,128]{2,0,1:T(8,128)} %copy.36), calls=%async_computation.4 | async-start | bytes 8388608 | tf_op jit(solution)/shard_map/all_to_all | solution.py:140
  1187.0 53.3 %all-to-all-start.3 = ((f32[64,128,128]{2,0,1:T(8,128)}), f32[64,128,128]{2,0,1:T(8,128)}, u32[]{:S(2)}, u32[]{:S(2)}) async-start(f32[64,128,128]{2,0,1:T(8,128)} %copy.34), calls=%async_computation.3 | async-start | bytes 8388608 | tf_op jit(solution)/shard_map/all_to_all | solution.py:139
  1287.4 98.5 %all-to-all-start.6 = ((f32[8,1,131072]{2,1,0:T(1,128)}), f32[8,1,131072]{2,1,0:T(1,128)}, u32[]{:S(2)}, u32[]{:S(2)}) async-start(f32[8,1,131072]{2,1,0:T(1,128)} %reshape.179), calls=%async_computation.6 | async-start | bytes 8388608 | tf_op jit(solution)/shard_map/all_to_all | solution.py:146
  1385.9 97.1 %all-to-all-start.5 = ((f32[8,1,131072]{2,1,0:T(1,128)}), f32[8,1,131072]{2,1,0:T(1,128)}, u32[]{:S(2)}, u32[]{:S(2)}) async-start(f32[8,1,131072]{2,1,0:T(1,128)} %reshape.177), calls=%async_computation.5 | async-start | bytes 8388608 | tf_op jit(solution)/shard_map/all_to_all | solution.py:145
  1393.9 4.4 collective-permute-start.7
  1394.0 168.8 %collective-permute-start.8 = (f32[1,64,512]{2,1,0:T(8,128)S(1)}, f32[1,64,512]{2,1,0:T(8,128)S(1)}, u32[]{:S(2)}, u32[]{:S(2)}) collective-permute-start(f32[1,64,512]{2,1,0:T(8,128)S(1)} %get-tuple-element.49), channel_id=1, source_target_pairs={{8,0},{16,8},{24,16},{0,24},{9,1},{17,9},{25,17},{1,25},{10,2},{18... | collective-permute-start | bytes 393224 | tf_op jit(solution)/shard_map/ppermute | solution.py:47
  1560.3 4.4 collective-permute-start.11
  1560.3 4.7 collective-permute-start.12
  1565.2 6.2 collective-permute-start.13
  1565.9 6.5 collective-permute-start.14
  1568.9 5.1 collective-permute-start.10
  1570.9 6.0 collective-permute-start.9
  1609.1 4.4 collective-permute-start.15
  1609.2 4.5 collective-permute-start.16
  1615.0 5.9 collective-permute-start.17
  1615.1 6.4 collective-permute-start.18
  1641.3 4.4 collective-permute-start.19
  1641.5 4.7 collective-permute-start.20
  1646.3 5.9 collective-permute-start.21
  1646.9 6.5 collective-permute-start.22
  (14 other events, 196.6 us)
